TPU v7x, 32 devices: a whole 2x2x4 slice. The times are simulated.
32 devices in a mesh: groups: 2 (over x), expert: 16 (over z, y, core), node: 1.
Axes of the slice: x: 2, y: 2, z: 4, core: 2. Of those that a mesh axis runs over, the one named last changes fastest.
Arguments:
- tokens: bfloat16 [2048, 7168], P(('groups', 'expert'), 'node'), parts along dimension 0, may hold values from -6 to 6
- expert_ids: int32 [2048, 8], P(('groups', 'expert')), parts along dimension 0, may hold values from 0 to 15, all different within a row; in each aligned block of 64 rows (0 to 63, 64 to 127, ...) at most 40 rows name the same one
- gate_values: float32 [2048, 8], P(('groups', 'expert')), parts along dimension 0, may hold values from 0.05 to 1
- gate_weight: bfloat16 [16, 7168, 1024], P('expert', None, 'node'), may hold values from -1 to 1
- up_weight: bfloat16 [16, 7168, 1024], P('expert', None, 'node'), may hold values from -1 to 1
- down_weight: bfloat16 [16, 1024, 7168], P('expert', 'node'), may hold values from -1 to 1
- sketch: bfloat16 [7168, 512], P('node'), may hold values from -0.0625 to 0.0625
- subsets: int32 [64, 8], replicated, may hold values from 0 to 15, as said below
Outputs:
- combined: bfloat16 [2048, 512], P(('groups', 'expert'), 'node'), parts along dimension 0
- gram_matrix: float32 [32, 16], P('groups'), parts along dimension 0
- prune_error: float32 [128], P('groups'), parts along dimension 0
There are 2 independent parts, one for each index of `groups`. A program takes and returns all parts, laid end to end along the dimension named above; an argument that names none is the same for every part. Nothing has to cross between parts.
Inputs may be any that keep to these rules, and one draw needn't show every extreme that they name: `expert_ids`: the ids of one token are distinct; among the 64 tokens of each aligned block no expert is chosen more than 40 times, a bound that some block reaches. `subsets`: each row names 8 different experts.
All inputs are finite; a program needn't handle non-finite values.
Results may differ from a plain program's by a relative error of at most 0.008.
Values may be sent and summed in bfloat16 or wider, within the bound.
A program may use at most 128 MiB of HBM per device.

v0:
```python
import jax
import jax.numpy as jnp
from jax import lax
from jax.sharding import PartitionSpec as P


def shards(tokens, expert_ids, gate_values, gate_weight, up_weight, down_weight, sketch, subsets):
    experts = lax.axis_size("expert")
    tok_rows = expert_ids.shape[0]
    top_count = expert_ids.shape[1]
    capacity = min(tok_rows, tok_rows * top_count * 5 // (4 * experts))
    flat_ids = expert_ids.reshape(-1)
    pick_count = flat_ids.shape[0]
    labels = jnp.arange(experts, dtype=jnp.int32)
    member = (flat_ids[:, None] == labels[None, :]).astype(jnp.int32)
    position = jnp.sum((jnp.cumsum(member, axis=0) - 1) * member, axis=1)
    slot_index = flat_ids * capacity + position
    source_row = jnp.arange(pick_count, dtype=jnp.int32) // top_count
    row_table = jnp.zeros((experts * capacity,), jnp.int32).at[slot_index].set(source_row)
    filled = jnp.zeros((experts * capacity,), jnp.bfloat16).at[slot_index].set(1.0)
    whole_rows = lax.all_gather(tokens, "node", axis=1, tiled=True)
    picked = jnp.take(whole_rows, row_table, axis=0) * filled[:, None]
    arrived = lax.all_to_all(
        picked.reshape(experts, capacity, whole_rows.shape[1]),
        "expert",
        split_axis=0,
        concat_axis=0,
        tiled=True,
    )
    model_width = arrived.shape[2]
    slot_rows = arrived.reshape(-1, model_width)
    down_local = down_weight[0]
    sketch_width = sketch.shape[1]
    sketched_down = jnp.dot(
        down_local,
        lax.all_gather(sketch, "node", axis=0, tiled=True),
        preferred_element_type=jnp.float32,
    ).astype(jnp.bfloat16)
    gate_part = jnp.dot(slot_rows, gate_weight[0], preferred_element_type=jnp.float32)
    up_part = jnp.dot(slot_rows, up_weight[0], preferred_element_type=jnp.float32)
    hidden = (jax.nn.silu(gate_part) * up_part).astype(jnp.bfloat16)
    partial_sketch = jnp.dot(hidden, sketched_down, preferred_element_type=jnp.float32)
    returned = lax.all_to_all(
        partial_sketch.reshape(experts, capacity, sketch_width),
        "expert",
        split_axis=0,
        concat_axis=0,
        tiled=True,
    )
    slot_sketch = lax.psum_scatter(returned, "node", scatter_dimension=2, tiled=True).astype(
        jnp.bfloat16
    )
    half_width = slot_sketch.shape[2]
    pick_sketch = jnp.take(slot_sketch.reshape(-1, half_width), slot_index, axis=0)
    pick_sketch = pick_sketch.reshape(tok_rows, top_count, half_width).astype(jnp.float32)
    combined = jnp.einsum("tk,tkc->tc", gate_values, pick_sketch).astype(jnp.bfloat16)
    gated_sketch = gate_values[:, :, None] * pick_sketch
    pair_inner = jnp.einsum("tkc,tlc->tkl", gated_sketch, gated_sketch)
    routing = (expert_ids[:, :, None] == labels[None, None, :]).astype(jnp.float32)
    local_gram = jnp.einsum("tke,tkl,tlf->ef", routing, pair_inner, routing)
    total_gram = lax.psum(local_gram, ("expert", "node"))
    gram_matrix = total_gram / (tok_rows * experts * sketch_width)
    kept_mask = jnp.sum((subsets[:, :, None] == labels[None, None, :]).astype(jnp.float32), axis=1)
    pruned = 1.0 - kept_mask
    prune_error = jnp.einsum("se,ef,sf->s", pruned, gram_matrix, pruned) / jnp.sum(gram_matrix)
    return (combined, gram_matrix, prune_error)


def solution(mesh):
    in_specs = (
        P(("groups", "expert"), "node"),
        P(("groups", "expert"), None),
        P(("groups", "expert"), None),
        P("expert", None, "node"),
        P("expert", None, "node"),
        P("expert", "node", None),
        P("node", None),
        P(),
    )
    out_specs = (P(("groups", "expert"), "node"), P("groups", None), P("groups"))
    return jax.shard_map(shards, mesh=mesh, in_specs=in_specs, out_specs=out_specs, check_vma=False)
```

profile of v0, /device:TPU:0, one launch (start us, length us, event | category | flops | bytes accessed | tf_op | source)
XLA Modules:
  0.0 328.6 jit_solution(6537191686353161520)
XLA Ops:
  0.6 0.9 copy.28
  1.5 0.1 eq.52
  1.6 0.1 reshape.100
  1.7 0.7 broadcast_multiply_fusion.1
  2.4 1.2 reduce-window.6
  3.5 0.2 slice_reduce_fusion
  3.9 0.1 mul.51
  4.0 0.1 fusion.32
  4.1 2.4 scatter_custom_fusion
  6.6 0.1 broadcast_in_dim.44
  6.7 3.8 %scatter_custom_fusion.1 = bf16[640]{0:T(1024)(128)(2,1)S(1)} fusion(s32[512]{0:T(512)S(1)} %bitcast.68, bf16[512]{0:T(512)(128)(2,1)S(1)} %broadcast.92, bf16[]{:T(256)} %constant.67.clone.1), kind=kCustom, calls=%fused_computation.61 | custom fusion | bytes 1282 | tf_op jit(solution)/shard_map/scatter | solution.py:20
  10.6 8.9 %gather_fusion = bf16[640,7168]{1,0:T(8,128)(2,1)} fusion(bf16[64,7168]{1,0:T(8,128)(2,1)S(1)} %copy-done, s32[1024]{0:T(1024)S(1)} %pad_clamp_fusion.1), kind=kCustom, calls=%fused_computation | custom fusion | bytes 18352640 | tf_op jit(solution)/shard_map/jit(_take)/gather | solution.py:22
  19.5 8.1 %select_multiply_fusion = bf16[16,40,7168]{2,1,0:T(8,128)(2,1)} fusion(bf16[16,40,7168]{2,1,0:T(8,128)(2,1)} %bitcast.62, pred[16,40]{1,0:T(8,128)(4,1)S(1)} %broadcast_in_dim.44, bf16[16,40]{1,0:T(8,128)(2,1)S(1)} %mul.52), kind=kLoop, calls=%fused_computation.10 | loop fusion | flops 9175040 | bytes 18352000 | tf_op jit(solution)/shard_map/mul | solution.py:22
  27.6 7.4 %all-to-all-start = ((bf16[16,40,7168]{2,1,0:T(8,128)(2,1)}), bf16[16,40,7168]{2,1,0:T(8,128)(2,1)}, u32[]{:S(2)}, u32[]{:S(2)}) async-start(bf16[16,40,7168]{2,1,0:T(8,128)(2,1)} %select_multiply_fusion), calls=%async_computation | async-start | bytes 18350080 | tf_op jit(solution)/shard_map/all_to_all | solution.py:23
  35.0 13.1 %fusion.11 = bf16[1024,512]{1,0:T(8,128)(2,1)S(1)} fusion(bf16[7168,512]{1,0:T(8,128)(2,1)} %param.14, bf16[1,1024,7168]{2,1,0:T(8,128)(2,1)} %param.13), kind=kOutput, calls=%fused_computation.13 | convolution fusion | flops 7516717056 | bytes 23068672 | tf_op jit(solution)/shard_map/dot_general | solution.py:34
  48.1 151.3 %all-to-all-done = bf16[16,40,7168]{2,1,0:T(8,128)(2,1)} async-done(((bf16[16,40,7168]{2,1,0:T(8,128)(2,1)}), bf16[16,40,7168]{2,1,0:T(8,128)(2,1)}, u32[]{:S(2)}, u32[]{:S(2)}) %all-to-all-start) | async-done | bytes 9175072 | tf_op jit(solution)/shard_map/all_to_all | solution.py:23
  199.4 15.8 %fusion.2 = f32[640,1024]{1,0:T(8,128)} fusion(bf16[640,7168]{1,0:T(8,128)(2,1)} %bitcast.5, bf16[1,7168,1024]{2,1,0:T(8,128)(2,1)} %param.12), kind=kOutput, calls=%fused_computation.6 | convolution fusion | flops 9395240960 | bytes 26476544 | tf_op jit(solution)/shard_map/dot_general | solution.py:40
  215.2 17.9 %fusion.9 = bf16[640,512]{1,0:T(8,128)(2,1)} fusion(bf16[1024,512]{1,0:T(8,128)(2,1)S(1)} %fusion.11, f32[640,1024]{1,0:T(8,128)} %fusion.2, bf16[640,7168]{1,0:T(8,128)(2,1)} %bitcast.5, bf16[1,7168,1024]{2,1,0:T(8,128)(2,1)} %param.11), kind=kOutput, calls=%fused_computation.12 | convolution fusion | flops 10070261760 | bytes 28180480 | tf_op jit(solution)/shard_map/dot_general | solution.py:42
  233.1 39.6 %all-to-all-start.1 = ((bf16[16,40,512]{2,1,0:T(8,128)(2,1)}), bf16[16,40,512]{2,1,0:T(8,128)(2,1)S(1)}, u32[]{:S(2)}, u32[]{:S(2)}) async-start(bf16[16,40,512]{2,1,0:T(8,128)(2,1)} %bitcast.9), calls=%async_computation.1 | async-start | bytes 1310720 | tf_op jit(solution)/shard_map/all_to_all | solution.py:43
  272.9 0.1 copy.32
  273.0 0.2 copy.36
  273.3 0.1 copy.38
  273.5 15.9 %all-to-all-done.1 = bf16[16,40,512]{2,1,0:T(8,128)(2,1)S(1)} async-done(((bf16[16,40,512]{2,1,0:T(8,128)(2,1)}), bf16[16,40,512]{2,1,0:T(8,128)(2,1)S(1)}, u32[]{:S(2)}, u32[]{:S(2)}) %all-to-all-start.1) | async-done | bytes 655392 | tf_op jit(solution)/shard_map/all_to_all | solution.py:43
  289.3 2.0 gather_fusion.1
  291.3 0.7 fusion.15
  292.0 0.2 convolution_bitcast_fusion.1
  292.2 33.3 %psum.7 = f32[16,16]{1,0:T(8,128)S(1)} all-reduce(f32[16,16]{1,0:T(8,128)S(1)} %convolution_bitcast_fusion.1), channel_id=1, replica_groups=mesh['groups'=2,'expert'=16,'node'=1] {'expert','node'}, use_global_device_ids=true, to_apply=%region_5.6 | all-reduce | flops 256 | bytes 2048 | tf_op jit(solution)/shard_map/psum | solution.py:61
  325.5 0.7 fusion.48
  326.1 0.4 fusion.26
  326.5 0.6 copy.51
  327.2 0.2 fusion.19
  327.3 1.2 broadcast_divide_fusion
  (30 shorter events, 0.6 us)
Async XLA Ops:
  0.6 9.9 %copy-start = (bf16[64,7168]{1,0:T(8,128)(2,1)S(1)}, bf16[64,7168]{1,0:T(8,128)(2,1)}, u32[]{:S(2)}) copy-start(bf16[64,7168]{1,0:T(8,128)(2,1)} %param.8) | copy-start | bytes 2752516
  27.6 171.8 %all-to-all-start = ((bf16[16,40,7168]{2,1,0:T(8,128)(2,1)}), bf16[16,40,7168]{2,1,0:T(8,128)(2,1)}, u32[]{:S(2)}, u32[]{:S(2)}) async-start(bf16[16,40,7168]{2,1,0:T(8,128)(2,1)} %select_multiply_fusion), calls=%async_computation | async-start | bytes 18350080 | tf_op jit(solution)/shard_map/all_to_all | solution.py:23
  215.2 57.7 %copy-start.2 = (s32[64,8]{0,1:T(8,128)S(1)}, s32[64,8]{0,1:T(8,128)}, u32[]{:S(2)}) copy-start(s32[64,8]{0,1:T(8,128)} %param.9) | copy-start | bytes 6148
  215.2 58.0 %copy-start.4 = (f32[64,8]{0,1:T(8,128)S(1)}, f32[64,8]{0,1:T(8,128)}, u32[]{:S(2)}) copy-start(f32[64,8]{0,1:T(8,128)} %param.10) | copy-start | bytes 6148
  215.2 58.2 %copy-start.5 = (s32[64,8]{0,1:T(8,128)S(1)}, s32[64,8]{0,1:T(8,128)}, u32[]{:S(2)}) copy-start(s32[64,8]{0,1:T(8,128)} %param.15) | copy-start | bytes 6148
  215.2 113.4 %copy-start.1 = (bf16[64,7168]{1,0:T(8,128)(2,1)S(1)}, bf16[64,7168]{1,0:T(8,128)(2,1)}, u32[]{:S(2)}) copy-start(bf16[64,7168]{1,0:T(8,128)(2,1)} %param.8) | copy-start | bytes 2752516
  233.1 56.3 %all-to-all-start.1 = ((bf16[16,40,512]{2,1,0:T(8,128)(2,1)}), bf16[16,40,512]{2,1,0:T(8,128)(2,1)S(1)}, u32[]{:S(2)}, u32[]{:S(2)}) async-start(bf16[16,40,512]{2,1,0:T(8,128)(2,1)} %bitcast.9), calls=%async_computation.1 | async-start | bytes 1310720 | tf_op jit(solution)/shard_map/all_to_all | solution.py:43
  326.1 2.4 copy-start.3
where the time goes:
time: 329 us
  waiting for transfers between devices  167 us (51%)
  matrix products  48.1 us (15%)
  starting transfers between devices  47.1 us (14%)
  blocking collectives  33.3 us (10%)
  local copies, waits for them, and re-layouts  20 us (6%)
  other arithmetic  12.1 us (4%)
    all_to_all x1, waiting for transfers between devices, shards(): lax.all_to_all(picked.reshape(experts, capacity, whole_rows.shape[1]), 'e...  151 us
    all_to_all x1, starting transfers between devices, shards(): lax.all_to_all(partial_sketch.reshape(experts, capacity, sketch_width), '...  39.6 us
    psum x1, blocking collectives, shards(): total_gram = lax.psum(local_gram, ('expert', 'node'))  33.3 us
    dot_general x1, matrix products, shards(): jnp.dot(hidden, sketched_down, preferred_element_type=jnp.float32)  17.9 us
    all_to_all x1, waiting for transfers between devices, shards(): lax.all_to_all(partial_sketch.reshape(experts, capacity, sketch_width), '...  15.9 us
    dot_general x1, matrix products, shards(): jnp.dot(slot_rows, up_weight[0], preferred_element_type=jnp.float32)  15.8 us
    dot_general x1, matrix products, shards(): jnp.dot(down_local, lax.all_gather(sketch, 'node', axis=0, tiled=True), p...  13.1 us
    gather x1, local copies, waits for them, and re-layouts, shards(): picked = jnp.take(whole_rows, row_table, axis=0) * filled[:, None]  8.89 us
  transfers between devices with their start and end apart: 2, of which 2 were waited for; matrix products, arithmetic and copies ran while one was open for 4% of the time, Pallas kernels for 0%

commit v1 on v0

--- a/solution.py
+++ b/solution.py
@@ -1,7 +1,402 @@
 import jax
 import jax.numpy as jnp
 from jax import lax
+from jax.experimental import pallas as pl
+from jax.experimental.pallas import tpu as pltpu
 from jax.sharding import PartitionSpec as P
+
+STEPS = 14
+LAG = 2
+ROW_TILE = 256
+
+
+def fused_kernel(
+    tokens,
+    ids,
+    gates,
+    gate_w,
+    up_w,
+    down_w,
+    sketch,
+    subsets,
+    combined,
+    gram_out,
+    prune_out,
+    xbuf,
+    acc_gate,
+    acc_up,
+    acc_down,
+    sd,
+    wbuf,
+    dbuf,
+    sbuf,
+    outbox,
+    inbox,
+    gated,
+    gram_box,
+    partial,
+    recv_sem,
+    up_sem,
+    down_sem,
+    side_sem,
+    core_sem,
+    w_sem,
+    d_sem,
+    back_send,
+    back_recv,
+    gram_send,
+    gram_recv,
+):
+    me = lax.axis_index("expert")
+    z, y, c = me // 4, (me // 2) % 2, me % 2
+    above, below = me + 4, me - 4
+    side = z * 4 + (1 - y) * 2 + c
+    twin = z * 4 + y * 2 + (1 - c)
+    rows, width = tokens.shape
+    chunk = width // STEPS
+    experts = 16
+
+    def to(device):
+        return {"expert": device}
+
+    def weight_loads(k):
+        slot = k % 2
+        at = pl.ds(pl.multiple_of(k * chunk, chunk), chunk)
+        return (
+            pltpu.make_async_copy(gate_w.at[at, :], wbuf.at[slot, 0], w_sem.at[slot, 0]),
+            pltpu.make_async_copy(up_w.at[at, :], wbuf.at[slot, 1], w_sem.at[slot, 1]),
+        )
+
+    def down_loads(k):
+        slot = k % 2
+        at = pl.ds(pl.multiple_of(k * chunk, chunk), chunk)
+        return (
+            pltpu.make_async_copy(down_w.at[:, at], dbuf.at[slot], d_sem.at[slot, 0]),
+            pltpu.make_async_copy(sketch.at[at, :], sbuf.at[slot], d_sem.at[slot, 1]),
+        )
+
+    for load in down_loads(0) + weight_loads(0):
+        load.start()
+
+    barrier = pltpu.get_barrier_semaphore()
+    for shift in range(1, experts):
+        pl.semaphore_signal(
+            barrier,
+            inc=1,
+            device_id=to((me + shift) % experts),
+            device_id_type=pl.DeviceIdType.MESH,
+        )
+    for k in range(STEPS):
+        xbuf[k, me] = tokens[:, k * chunk : (k + 1) * chunk]
+    acc_gate[...] = jnp.zeros_like(acc_gate)
+    acc_up[...] = jnp.zeros_like(acc_up)
+    acc_down[...] = jnp.zeros_like(acc_down)
+    pl.semaphore_wait(barrier, experts - 1)
+
+    def send(k, block, sem, target):
+        return pltpu.make_async_remote_copy(
+            src_ref=xbuf.at[k, block],
+            dst_ref=xbuf.at[k, block],
+            send_sem=sem,
+            recv_sem=recv_sem.at[k, block],
+            device_id=to(target),
+            device_id_type=pl.DeviceIdType.MESH,
+        )
+
+    def when_chunk(k, also=None):
+        cond = (k >= 0) & (k < STEPS)
+        return pl.when(cond if also is None else cond & also)
+
+    def step(s, carry):
+        for plane in range(4):
+            dist = jnp.abs(z - plane)
+            block = plane * 4 + y * 2 + c
+            k = s - LAG * dist
+
+            @when_chunk(k)
+            def _():
+                @pl.when(z != plane)
+                def _():
+                    send(k, block, up_sem.at[k, plane], twin).wait_recv()
+
+                @pl.when((plane <= z) & (z < 3))
+                def _():
+                    send(k, block, up_sem.at[k, plane], above).start()
+
+                @pl.when((plane >= z) & (z > 0))
+                def _():
+                    send(k, block, down_sem.at[k, plane], below).start()
+
+                send(k, block, side_sem.at[k, plane], side).start()
+                send(k, block, core_sem.at[k, plane], twin).start()
+
+        for plane in range(4):
+            dist = jnp.abs(z - plane)
+            block = plane * 4 + (1 - y) * 2 + c
+            k = s - LAG * (dist + 1)
+
+            @when_chunk(k)
+            def _():
+                send(k, block, core_sem.at[k, 4 + plane], twin).wait_recv()
+                send(k, block, core_sem.at[k, 4 + plane], twin).start()
+
+        @pl.when(s < STEPS)
+        def _():
+            slot = s % 2
+
+            @pl.when(s + 1 < STEPS)
+            def _():
+                for load in down_loads(s + 1):
+                    load.start()
+
+            for load in down_loads(s):
+                load.wait()
+
+            @pl.loop(0, down_w.shape[0] // ROW_TILE)
+            def _(r):
+                at = pl.ds(pl.multiple_of(r * ROW_TILE, ROW_TILE), ROW_TILE)
+                acc_down[at, :] += jnp.dot(
+                    dbuf[slot, at, :], sbuf[slot], preferred_element_type=jnp.float32
+                )
+
+        k = s - 5 * LAG
+
+        @when_chunk(k)
+        def _():
+            slot = k % 2
+
+            @pl.when(k + 1 < STEPS)
+            def _():
+                for load in weight_loads(k + 1):
+                    load.start()
+
+            for plane in range(4):
+                for col in range(2):
+                    block = plane * 4 + col * 2 + (1 - c)
+                    send(k, block, up_sem.at[k, plane], twin).wait_recv()
+            for load in weight_loads(k):
+                load.wait()
+
+            @pl.loop(0, experts * rows // ROW_TILE)
+            def _(r):
+                per = ROW_TILE // rows
+                at = pl.ds(pl.multiple_of(r * ROW_TILE, ROW_TILE), ROW_TILE)
+                x = xbuf[k, pl.ds(r * per, per)].reshape(ROW_TILE, chunk)
+                acc_gate[at, :] += jnp.dot(x, wbuf[slot, 0], preferred_element_type=jnp.float32)
+                acc_up[at, :] += jnp.dot(x, wbuf[slot, 1], preferred_element_type=jnp.float32)
+
+        return carry
+
+    lax.fori_loop(0, STEPS + 5 * LAG, step, 0)
+
+    sd[...] = acc_down[...].astype(jnp.bfloat16)
+
+    def back(block):
+        return pltpu.make_async_remote_copy(
+            src_ref=outbox.at[block],
+            dst_ref=inbox.at[me],
+            send_sem=back_send.at[block],
+            recv_sem=back_recv.at[me],
+            device_id=to(block),
+            device_id_type=pl.DeviceIdType.MESH,
+        )
+
+    def finish(i, carry):
+        plane = (z + 1 + i) % 4
+        at = pl.ds(pl.multiple_of(plane * 4 * rows, 4 * rows), 4 * rows)
+        g = acc_gate[at, :]
+        hidden = (g / (1.0 + jnp.exp(-g)) * acc_up[at, :]).astype(jnp.bfloat16)
+        result = jnp.dot(hidden, sd[...], preferred_element_type=jnp.float32).astype(jnp.bfloat16)
+        outbox[pl.ds(plane * 4, 4)] = result.reshape(4, rows, -1)
+        for j in range(4):
+            block = plane * 4 + j
+
+            @pl.when(block != me)
+            def _():
+                back(block).start()
+
+        return carry
+
+    lax.fori_loop(0, 4, finish, 0)
+    inbox[me] = outbox[me]
+
+    def arrived(e):
+        return pltpu.make_async_remote_copy(
+            src_ref=outbox.at[e],
+            dst_ref=inbox.at[e],
+            send_sem=back_send.at[e],
+            recv_sem=back_recv.at[e],
+            device_id=to(twin),
+            device_id_type=pl.DeviceIdType.MESH,
+        )
+
+    total = jnp.zeros(combined.shape, jnp.float32)
+    for e in range(experts):
+
+        @pl.when(me != e)
+        def _():
+            arrived(e).wait_recv()
+
+        gate = jnp.sum(jnp.where(ids[...] == e, gates[...], 0.0), axis=1, keepdims=True)
+        part = gate * inbox[e].astype(jnp.float32)
+        total = total + part
+        gated[e * rows : (e + 1) * rows, :] = part.astype(jnp.bfloat16)
+    combined[...] = total.astype(combined.dtype)
+
+    flat = experts * rows
+    tile = 4 * rows
+    row_tok = lax.broadcasted_iota(jnp.int32, (tile, flat), 0) % rows
+    col_tok = lax.broadcasted_iota(jnp.int32, (tile, flat), 1) % rows
+    same = row_tok == col_tok
+    for r in range(4):
+        pair = lax.dot_general(
+            gated[r * tile : (r + 1) * tile, :],
+            gated[...],
+            (((1,), (1,)), ((), ())),
+            preferred_element_type=jnp.float32,
+        )
+        pair = jnp.where(same, pair, 0.0).reshape(4, rows, flat)
+        partial[r * 4 : (r + 1) * 4, :] = jnp.sum(pair, axis=1)
+    owner = lax.broadcasted_iota(jnp.int32, (flat, experts), 0) // rows
+    label = lax.broadcasted_iota(jnp.int32, (flat, experts), 1)
+    local = jnp.dot(
+        partial[...],
+        (owner == label).astype(jnp.float32),
+        preferred_element_type=jnp.float32,
+        precision=lax.Precision.HIGHEST,
+    )
+    gram_box[me] = local
+
+    def share(shift):
+        other = (me + shift) % experts
+        return pltpu.make_async_remote_copy(
+            src_ref=gram_box.at[me],
+            dst_ref=gram_box.at[me],
+            send_sem=gram_send.at[shift],
+            recv_sem=gram_recv.at[me],
+            device_id=to(other),
+            device_id_type=pl.DeviceIdType.MESH,
+        )
+
+    def shared(e):
+        return pltpu.make_async_remote_copy(
+            src_ref=gram_box.at[e],
+            dst_ref=gram_box.at[e],
+            send_sem=gram_send.at[0],
+            recv_sem=gram_recv.at[e],
+            device_id=to(twin),
+            device_id_type=pl.DeviceIdType.MESH,
+        )
+
+    for shift in range(1, experts):
+        share(shift).start()
+    names = subsets[...]
+    columns = lax.broadcasted_iota(jnp.int32, (names.shape[0], experts), 1)
+    kept = jnp.zeros((names.shape[0], experts), jnp.float32)
+    for j in range(names.shape[1]):
+        kept = kept + jnp.where(names[:, j : j + 1] == columns, 1.0, 0.0)
+    pruned = 1.0 - kept
+
+    def collect(k, carry):
+        for plane in range(4):
+            block = plane * 4 + y * 2 + c
+            across = plane * 4 + (1 - y) * 2 + c
+
+            @pl.when((plane <= z) & (z < 3))
+            def _():
+                send(k, block, up_sem.at[k, plane], above).wait_send()
+
+            @pl.when((plane >= z) & (z > 0))
+            def _():
+                send(k, block, down_sem.at[k, plane], below).wait_send()
+
+            send(k, block, side_sem.at[k, plane], side).wait_send()
+            send(k, block, core_sem.at[k, plane], twin).wait_send()
+            send(k, across, core_sem.at[k, 4 + plane], twin).wait_send()
+        return carry
+
+    lax.fori_loop(0, STEPS, collect, 0)
+    for e in range(experts):
+
+        @pl.when(me != e)
+        def _():
+            arrived(e).wait_send()
+
+    for e in range(experts):
+
+        @pl.when(me != e)
+        def _():
+            shared(e).wait_recv()
+
+    gram = jnp.sum(gram_box[...], axis=0) / (rows * experts * sketch.shape[1])
+    gram_out[...] = gram
+    weighed = jnp.dot(
+        pruned, gram, preferred_element_type=jnp.float32, precision=lax.Precision.HIGHEST
+    )
+    prune_out[...] = jnp.sum(weighed * pruned, axis=1, keepdims=True) / jnp.sum(gram)
+    for shift in range(1, experts):
+        share(shift).wait_send()
+
+
+def fused(tokens, expert_ids, gate_values, gate_weight, up_weight, down_weight, sketch, subsets):
+    rows, width = tokens.shape
+    experts = 16
+    chunk = width // STEPS
+    hidden_width = gate_weight.shape[2]
+    sketch_width = sketch.shape[1]
+    bf16, f32 = jnp.bfloat16, jnp.float32
+    dma = pltpu.SemaphoreType.DMA
+    vmem = pl.BlockSpec(memory_space=pltpu.VMEM)
+    hbm = pl.BlockSpec(memory_space=pl.ANY)
+    combined, gram, prune = pl.pallas_call(
+        fused_kernel,
+        out_shape=(
+            jax.ShapeDtypeStruct((rows, sketch_width), bf16),
+            jax.ShapeDtypeStruct((experts, experts), f32),
+            jax.ShapeDtypeStruct((subsets.shape[0], 1), f32),
+        ),
+        in_specs=[vmem, vmem, vmem, hbm, hbm, hbm, hbm, vmem],
+        out_specs=(vmem, vmem, vmem),
+        scratch_shapes=[
+            pltpu.VMEM((STEPS, experts, rows, chunk), bf16),
+            pltpu.VMEM((experts * rows, hidden_width), f32),
+            pltpu.VMEM((experts * rows, hidden_width), f32),
+            pltpu.VMEM((hidden_width, sketch_width), f32),
+            pltpu.VMEM((hidden_width, sketch_width), bf16),
+            pltpu.VMEM((2, 2, chunk, hidden_width), bf16),
+            pltpu.VMEM((2, hidden_width, chunk), bf16),
+            pltpu.VMEM((2, chunk, sketch_width), bf16),
+            pltpu.VMEM((experts, rows, sketch_width), bf16),
+            pltpu.VMEM((experts, rows, sketch_width), bf16),
+            pltpu.VMEM((experts * rows, sketch_width), bf16),
+            pltpu.VMEM((experts, experts, experts), f32),
+            pltpu.VMEM((experts, experts * rows), f32),
+            dma((STEPS, experts)),
+            dma((STEPS, 4)),
+            dma((STEPS, 4)),
+            dma((STEPS, 4)),
+            dma((STEPS, 8)),
+            dma((2, 2)),
+            dma((2, 2)),
+            dma((experts,)),
+            dma((experts,)),
+            dma((experts,)),
+            dma((experts,)),
+        ],
+        compiler_params=pltpu.CompilerParams(
+            collective_id=0, has_side_effects=True, vmem_limit_bytes=58 * 1024 * 1024
+        ),
+    )(
+        tokens,
+        expert_ids,
+        gate_values,
+        gate_weight.reshape(gate_weight.shape[1:]),
+        up_weight.reshape(up_weight.shape[1:]),
+        down_weight.reshape(down_weight.shape[1:]),
+        sketch,
+        subsets,
+    )
+    return combined, gram, prune.reshape(-1)
 
 
 def shards(tokens, expert_ids, gate_values, gate_weight, up_weight, down_weight, sketch, subsets):
@@ -78,4 +473,5 @@
         P(),
     )
     out_specs = (P(("groups", "expert"), "node"), P("groups", None), P("groups"))
-    return jax.shard_map(shards, mesh=mesh, in_specs=in_specs, out_specs=out_specs, check_vma=False)
+    plain = mesh.shape["node"] == 1 and mesh.shape["expert"] == 16
+    return jax.shard_map(fused if plain else shards, mesh=mesh, in_specs=in_specs, out_specs=out_specs, check_vma=False)

time: 329 us -> 153 us (0.47)
  waiting for transfers between devices: 167 us -> 0 us
  Pallas kernels: 0 us -> 144 us
  matrix products: 48.1 us -> 0 us
  starting transfers between devices: 47.1 us -> 0 us
  blocking collectives: 33.3 us -> 0 us
  local copies, waits for them, and re-layouts: 20 us -> 6.89 us
  other arithmetic: 12.1 us -> 1.39 us
    all_to_all x2 -> x0, waiting for transfers between devices: 167 us -> none  [the longest x1 151 us: shards(): lax.all_to_all(picked.reshape(experts, capacity, whole_rows.shape[1]), 'e...]
    pallas_call x0 -> x1, Pallas kernels: none -> 144 us  [fused(): pl.pallas_call(fused_kernel, out_shape=(jax.ShapeDtypeStruct((rows, sketc...]
    dot_general x7 -> x0, matrix products: 48.1 us -> none  [the longest x1 17.9 us: shards(): jnp.dot(hidden, sketched_down, preferred_element_type=jnp.float32)]
    all_to_all x2 -> x0, starting transfers between devices: 47.1 us -> none  [the longest x1 39.6 us: shards(): lax.all_to_all(partial_sketch.reshape(experts, capacity, sketch_width), '...]
    psum x1 -> x0, blocking collectives: 33.3 us -> none  [shards(): total_gram = lax.psum(local_gram, ('expert', 'node'))]
    gather x2 -> x0, local copies, waits for them, and re-layouts: 10.8 us -> none  [the longest x1 8.89 us: shards(): picked = jnp.take(whole_rows, row_table, axis=0) * filled[:, None]]
    mul x2 -> x0, other arithmetic: 8.82 us -> none  [the longest x1 8.13 us: shards(): picked = jnp.take(whole_rows, row_table, axis=0) * filled[:, None]]
    scatter x2 -> x0, local copies, waits for them, and re-layouts: 6.21 us -> none  [the longest x1 3.77 us: shards(): jnp.zeros((experts * capacity,), jnp.bfloat16).at[slot_index].set(1.0)]
  transfers between devices with their start and end apart: 2 -> 0, of which waited for: 2 -> 0; matrix products, arithmetic and copies ran while one was open for 4% -> 0% of each run, Pallas kernels for 0% -> 0%
where the time goes in v1:
time: 153 us
  Pallas kernels  144 us (94%)
  local copies, waits for them, and re-layouts  6.89 us (5%)
    pallas_call x1, Pallas kernels, fused(): pl.pallas_call(fused_kernel, out_shape=(jax.ShapeDtypeStruct((rows, sketc...  144 us
    unnamed x5, local copies, waits for them, and re-layouts  6.89 us

profile of v1, /device:TPU:0, one launch (start us, length us, event | category | flops | bytes accessed | tf_op | source)
XLA Modules:
  0.0 152.6 jit_solution(9524868655127145605)
XLA Ops:
  0.6 1.4 copy.14.ids
  2.0 1.4 copy.15.gates
  3.4 1.4 copy.16.subsets
  4.8 143.7 %shard_map.103 = (bf16[64,512]{1,0:T(8,128)(2,1)}, f32[16,16]{1,0:T(8,128)}, f32[64,1]{1,0:T(8,128)}) custom-call(bf16[64,7168]{1,0:T(8,128)(2,1)} %tokens.1, s32[64,8]{1,0:T(8,128)} %copy.14.ids, f32[64,8]{1,0:T(8,128)} %copy.15.gates, bf16[7168,1024]{1,0:T(8,128)(2,1)} %bitcast.3, bf16[7168,1024]{1,0:T(8,128)(2,1)} %bitcast.4, bf16[1024,7168]{1,0:T(8,128)(2,1)} %bitcast.5, ...), custom_call_target="tpu_custom_call" | custom-call | tf_op jit(solution)/shard_map/pallas_call | solution.py:351
  148.4 1.4 reduce
  149.8 1.5 copy.19
  151.3 1.3 copy.20

commit v2 on v1

--- a/solution.py
+++ b/solution.py
@@ -6,7 +6,8 @@
 from jax.sharding import PartitionSpec as P
 
 STEPS = 14
-LAG = 2
+LAG = 1
+BOTH = 7
 ROW_TILE = 256
 
 
@@ -42,6 +43,12 @@
     core_sem,
     w_sem,
     d_sem,
+    slots_out,
+    slots_in,
+    cross_up,
+    cross_down,
+    slot_send,
+    slot_recv,
     back_send,
     back_recv,
     gram_send,
@@ -91,6 +98,38 @@
     acc_gate[...] = jnp.zeros_like(acc_gate)
     acc_up[...] = jnp.zeros_like(acc_up)
     acc_down[...] = jnp.zeros_like(acc_down)
+
+    capacity = outbox.shape[1] // 2
+    lanes = lax.broadcasted_iota(jnp.int32, (rows, experts), 1)
+    member = jnp.zeros((rows, experts), jnp.float32)
+    for j in range(ids.shape[1]):
+        member = member + jnp.where(ids[:, j : j + 1] == lanes, 1.0, 0.0)
+    member = member.astype(jnp.bfloat16)
+    first = lax.broadcasted_iota(jnp.int32, (rows, 2 * rows), 0)
+    second = lax.broadcasted_iota(jnp.int32, (rows, 2 * rows), 1) % rows
+
+    def turned(mask):
+        return lax.dot_general(
+            member,
+            jnp.where(mask, 1.0, 0.0).astype(jnp.bfloat16),
+            (((0,), (0,)), ((), ())),
+            preferred_element_type=jnp.float32,
+        )
+
+    slots = jnp.where(turned(first == second) > 0.5, turned(first < second), -1.0)
+    for e in range(experts):
+        slots_out[e] = jnp.broadcast_to(slots[e : e + 1, :], (8, 2 * rows))
+    slots_in[me] = slots_out[me]
+
+    def picker(row):
+        shape = (2 * capacity, 2 * rows)
+        place = lax.broadcasted_iota(jnp.int32, shape, 0)
+        half = lax.broadcasted_iota(jnp.int32, shape, 1) >= rows
+        late = place >= capacity
+        wanted = jnp.where(late, place - capacity, place).astype(jnp.float32)
+        wanted = jnp.where(late == half, wanted, -2.0)
+        return jnp.where(row == wanted, 1.0, 0.0).astype(jnp.bfloat16)
+
     pl.semaphore_wait(barrier, experts - 1)
 
     def send(k, block, sem, target):
@@ -103,6 +142,32 @@
             device_id_type=pl.DeviceIdType.MESH,
         )
 
+    def slot_copy(block):
+        return pltpu.make_async_remote_copy(
+            src_ref=slots_out.at[block],
+            dst_ref=slots_in.at[me],
+            send_sem=slot_send.at[block],
+            recv_sem=slot_recv.at[me],
+            device_id=to(block),
+            device_id_type=pl.DeviceIdType.MESH,
+        )
+
+    def slot_arrived(e):
+        return pltpu.make_async_remote_copy(
+            src_ref=slots_out.at[e],
+            dst_ref=slots_in.at[e],
+            send_sem=slot_send.at[e],
+            recv_sem=slot_recv.at[e],
+            device_id=to(twin),
+            device_id_type=pl.DeviceIdType.MESH,
+        )
+
+    for e in range(experts):
+
+        @pl.when(me != e)
+        def _():
+            slot_copy(e).start()
+
     def when_chunk(k, also=None):
         cond = (k >= 0) & (k < STEPS)
         return pl.when(cond if also is None else cond & also)
@@ -127,7 +192,10 @@
                 def _():
                     send(k, block, down_sem.at[k, plane], below).start()
 
-                send(k, block, side_sem.at[k, plane], side).start()
+                @pl.when((z == plane) | (k % BOTH != 0))
+                def _():
+                    send(k, block, side_sem.at[k, plane], side).start()
+
                 send(k, block, core_sem.at[k, plane], twin).start()
 
         for plane in range(4):
@@ -138,6 +206,15 @@
             @when_chunk(k)
             def _():
                 send(k, block, core_sem.at[k, 4 + plane], twin).wait_recv()
+
+                @pl.when((plane <= z) & (z < 3) & (k % BOTH == 0))
+                def _():
+                    send(k, block, cross_up.at[k, plane], above).start()
+
+                @pl.when((plane >= z) & (z > 0) & (k % BOTH == 0))
+                def _():
+                    send(k, block, cross_down.at[k, plane], below).start()
+
                 send(k, block, core_sem.at[k, 4 + plane], twin).start()
 
         @pl.when(s < STEPS)
@@ -191,6 +268,14 @@
 
     sd[...] = acc_down[...].astype(jnp.bfloat16)
 
+    for e in range(experts):
+
+        @pl.when(me != e)
+        def _():
+            slot_arrived(e).wait_recv()
+
+    half_width = sd.shape[1] // 2
+
     def back(block):
         return pltpu.make_async_remote_copy(
             src_ref=outbox.at[block],
@@ -207,9 +292,13 @@
         g = acc_gate[at, :]
         hidden = (g / (1.0 + jnp.exp(-g)) * acc_up[at, :]).astype(jnp.bfloat16)
         result = jnp.dot(hidden, sd[...], preferred_element_type=jnp.float32).astype(jnp.bfloat16)
-        outbox[pl.ds(plane * 4, 4)] = result.reshape(4, rows, -1)
         for j in range(4):
             block = plane * 4 + j
+            mine = result[j * rows : (j + 1) * rows]
+            mine = jnp.concatenate([mine[:, :half_width], mine[:, half_width:]], axis=0)
+            outbox[block] = jnp.dot(
+                picker(slots_in[block][0:1, :]), mine, preferred_element_type=jnp.float32
+            ).astype(jnp.bfloat16)
 
             @pl.when(block != me)
             def _():
@@ -238,7 +327,13 @@
             arrived(e).wait_recv()
 
         gate = jnp.sum(jnp.where(ids[...] == e, gates[...], 0.0), axis=1, keepdims=True)
-        part = gate * inbox[e].astype(jnp.float32)
+        spread = lax.dot_general(
+            picker(slots_out[e][0:1, :]),
+            inbox[e],
+            (((0,), (0,)), ((), ())),
+            preferred_element_type=jnp.float32,
+        )
+        part = gate * jnp.concatenate([spread[:rows], spread[rows:]], axis=1)
         total = total + part
         gated[e * rows : (e + 1) * rows, :] = part.astype(jnp.bfloat16)
     combined[...] = total.astype(combined.dtype)
@@ -310,7 +405,18 @@
             def _():
                 send(k, block, down_sem.at[k, plane], below).wait_send()
 
-            send(k, block, side_sem.at[k, plane], side).wait_send()
+            @pl.when((z == plane) | (k % BOTH != 0))
+            def _():
+                send(k, block, side_sem.at[k, plane], side).wait_send()
+
+            @pl.when((plane <= z) & (z < 3) & (k % BOTH == 0))
+            def _():
+                send(k, across, cross_up.at[k, plane], above).wait_send()
+
+            @pl.when((plane >= z) & (z > 0) & (k % BOTH == 0))
+            def _():
+                send(k, across, cross_down.at[k, plane], below).wait_send()
+
             send(k, block, core_sem.at[k, plane], twin).wait_send()
             send(k, across, core_sem.at[k, 4 + plane], twin).wait_send()
         return carry
@@ -321,6 +427,7 @@
         @pl.when(me != e)
         def _():
             arrived(e).wait_send()
+            slot_arrived(e).wait_send()
 
     for e in range(experts):
 
@@ -342,6 +449,7 @@
     rows, width = tokens.shape
     experts = 16
     chunk = width // STEPS
+    capacity = min(rows, rows * expert_ids.shape[1] * 5 // (4 * experts))
     hidden_width = gate_weight.shape[2]
     sketch_width = sketch.shape[1]
     bf16, f32 = jnp.bfloat16, jnp.float32
@@ -366,8 +474,8 @@
             pltpu.VMEM((2, 2, chunk, hidden_width), bf16),
             pltpu.VMEM((2, hidden_width, chunk), bf16),
             pltpu.VMEM((2, chunk, sketch_width), bf16),
-            pltpu.VMEM((experts, rows, sketch_width), bf16),
-            pltpu.VMEM((experts, rows, sketch_width), bf16),
+            pltpu.VMEM((experts, 2 * capacity, sketch_width // 2), bf16),
+            pltpu.VMEM((experts, 2 * capacity, sketch_width // 2), bf16),
             pltpu.VMEM((experts * rows, sketch_width), bf16),
             pltpu.VMEM((experts, experts, experts), f32),
             pltpu.VMEM((experts, experts * rows), f32),
@@ -378,6 +486,12 @@
             dma((STEPS, 8)),
             dma((2, 2)),
             dma((2, 2)),
+            pltpu.VMEM((experts, 8, 2 * rows), f32),
+            pltpu.VMEM((experts, 8, 2 * rows), f32),
+            dma((STEPS, 4)),
+            dma((STEPS, 4)),
+            dma((experts,)),
+            dma((experts,)),
             dma((experts,)),
             dma((experts,)),
             dma((experts,)),

time: 153 us -> 141 us (0.922)
  Pallas kernels: 144 us -> 131 us
    pallas_call x1, Pallas kernels: 144 us -> 131 us  [fused(): pl.pallas_call(fused_kernel, out_shape=(jax.ShapeDtypeStruct((rows, sketc...]
where the time goes in v2:
time: 141 us; the launch traced here: 140 us
  Pallas kernels  131 us (93%)
  local copies, waits for them, and re-layouts  6.89 us (5%)
    pallas_call x1, Pallas kernels, fused(): pl.pallas_call(fused_kernel, out_shape=(jax.ShapeDtypeStruct((rows, sketc...  131 us
    unnamed x5, local copies, waits for them, and re-layouts  6.89 us

profile of v2, /device:TPU:0, one launch (start us, length us, event | category | flops | bytes accessed | tf_op | source)
XLA Modules:
  0.0 140.2 jit_solution(13599173794174664213)
XLA Ops:
  0.6 1.4 copy.14.ids
  2.0 1.4 copy.15.gates
  3.4 1.4 copy.16.subsets
  4.8 131.3 %shard_map.103 = (bf16[64,512]{1,0:T(8,128)(2,1)}, f32[16,16]{1,0:T(8,128)}, f32[64,1]{1,0:T(8,128)}) custom-call(bf16[64,7168]{1,0:T(8,128)(2,1)} %tokens.1, s32[64,8]{1,0:T(8,128)} %copy.14.ids, f32[64,8]{1,0:T(8,128)} %copy.15.gates, bf16[7168,1024]{1,0:T(8,128)(2,1)} %bitcast.3, bf16[7168,1024]{1,0:T(8,128)(2,1)} %bitcast.4, bf16[1024,7168]{1,0:T(8,128)(2,1)} %bitcast.5, ...), custom_call_target="tpu_custom_call" | custom-call | tf_op jit(solution)/shard_map/pallas_call | solution.py:459
  136.0 1.4 reduce
  137.4 1.5 %copy.19 = bf16[64,512]{1,0:T(8,128)(2,1)} copy(bf16[64,512]{1,0:T(8,128)(2,1)} %get-tuple-element.12) | data formatting | bytes 131072
  138.9 1.3 copy.20

commit v3 on v2

--- a/solution.py
+++ b/solution.py
@@ -100,10 +100,13 @@
     acc_down[...] = jnp.zeros_like(acc_down)
 
     capacity = outbox.shape[1] // 2
-    lanes = lax.broadcasted_iota(jnp.int32, (rows, experts), 1)
-    member = jnp.zeros((rows, experts), jnp.float32)
-    for j in range(ids.shape[1]):
-        member = member + jnp.where(ids[:, j : j + 1] == lanes, 1.0, 0.0)
+    labels = lax.broadcasted_iota(jnp.int32, (experts, rows), 0)
+    member = jnp.zeros((experts, rows), jnp.float32)
+    gate_of = jnp.zeros((experts, rows), jnp.float32)
+    for j in range(ids.shape[0]):
+        named = ids[j : j + 1, :] == labels
+        member = member + jnp.where(named, 1.0, 0.0)
+        gate_of = gate_of + jnp.where(named, gates[j : j + 1, :], 0.0)
     member = member.astype(jnp.bfloat16)
     first = lax.broadcasted_iota(jnp.int32, (rows, 2 * rows), 0)
     second = lax.broadcasted_iota(jnp.int32, (rows, 2 * rows), 1) % rows
@@ -112,7 +115,7 @@
         return lax.dot_general(
             member,
             jnp.where(mask, 1.0, 0.0).astype(jnp.bfloat16),
-            (((0,), (0,)), ((), ())),
+            (((1,), (0,)), ((), ())),
             preferred_element_type=jnp.float32,
         )
 
@@ -319,6 +322,9 @@
             device_id_type=pl.DeviceIdType.MESH,
         )
 
+    same_token = lax.broadcasted_iota(jnp.int32, (rows, rows), 0) == lax.broadcasted_iota(
+        jnp.int32, (rows, rows), 1
+    )
     total = jnp.zeros(combined.shape, jnp.float32)
     for e in range(experts):
 
@@ -326,7 +332,7 @@
         def _():
             arrived(e).wait_recv()
 
-        gate = jnp.sum(jnp.where(ids[...] == e, gates[...], 0.0), axis=1, keepdims=True)
+        gate = jnp.sum(jnp.where(same_token, gate_of[e : e + 1, :], 0.0), axis=1, keepdims=True)
         spread = lax.dot_general(
             picker(slots_out[e][0:1, :]),
             inbox[e],
@@ -386,10 +392,10 @@
     for shift in range(1, experts):
         share(shift).start()
     names = subsets[...]
-    columns = lax.broadcasted_iota(jnp.int32, (names.shape[0], experts), 1)
-    kept = jnp.zeros((names.shape[0], experts), jnp.float32)
-    for j in range(names.shape[1]):
-        kept = kept + jnp.where(names[:, j : j + 1] == columns, 1.0, 0.0)
+    columns = lax.broadcasted_iota(jnp.int32, (experts, names.shape[1]), 0)
+    kept = jnp.zeros((experts, names.shape[1]), jnp.float32)
+    for j in range(names.shape[0]):
+        kept = kept + jnp.where(names[j : j + 1, :] == columns, 1.0, 0.0)
     pruned = 1.0 - kept
 
     def collect(k, carry):
@@ -438,9 +444,9 @@
     gram = jnp.sum(gram_box[...], axis=0) / (rows * experts * sketch.shape[1])
     gram_out[...] = gram
     weighed = jnp.dot(
-        pruned, gram, preferred_element_type=jnp.float32, precision=lax.Precision.HIGHEST
-    )
-    prune_out[...] = jnp.sum(weighed * pruned, axis=1, keepdims=True) / jnp.sum(gram)
+        gram, pruned, preferred_element_type=jnp.float32, precision=lax.Precision.HIGHEST
+    )
+    prune_out[...] = jnp.sum(weighed * pruned, axis=0, keepdims=True) / jnp.sum(gram)
     for shift in range(1, experts):
         share(shift).wait_send()
 
@@ -461,7 +467,7 @@
         out_shape=(
             jax.ShapeDtypeStruct((rows, sketch_width), bf16),
             jax.ShapeDtypeStruct((experts, experts), f32),
-            jax.ShapeDtypeStruct((subsets.shape[0], 1), f32),
+            jax.ShapeDtypeStruct((1, subsets.shape[0]), f32),
         ),
         in_specs=[vmem, vmem, vmem, hbm, hbm, hbm, hbm, vmem],
         out_specs=(vmem, vmem, vmem),
@@ -502,13 +508,13 @@
         ),
     )(
         tokens,
-        expert_ids,
-        gate_values,
+        expert_ids.T,
+        gate_values.T,
         gate_weight.reshape(gate_weight.shape[1:]),
         up_weight.reshape(up_weight.shape[1:]),
         down_weight.reshape(down_weight.shape[1:]),
         sketch,
-        subsets,
+        subsets.T,
     )
     return combined, gram, prune.reshape(-1)
 

time: 141 us -> 136 us (0.965)
  local copies, waits for them, and re-layouts: 6.89 us -> 3.88 us
    unnamed x5 -> x3, local copies, waits for them, and re-layouts: 6.89 us -> 3.88 us
where the time goes in v3:
time: 136 us
  Pallas kernels  131 us (96%)
  local copies, waits for them, and re-layouts  3.88 us (3%)
    pallas_call x1, Pallas kernels, fused(): pl.pallas_call(fused_kernel, out_shape=(jax.ShapeDtypeStruct((rows, sketc...  131 us
    unnamed x3, local copies, waits for them, and re-layouts  3.88 us

profile of v3, /device:TPU:0, one launch (start us, length us, event | category | flops | bytes accessed | tf_op | source)
XLA Modules:
  0.0 135.6 jit_solution(7105552962665321713)
XLA Ops:
  0.6 131.1 %shard_map.103 = (bf16[64,512]{1,0:T(8,128)(2,1)}, f32[16,16]{1,0:T(8,128)}, f32[1,64]{1,0:T(1,128)}) custom-call(bf16[64,7168]{1,0:T(8,128)(2,1)} %tokens.1, s32[8,64]{1,0:T(8,128)} %bitcast.10, f32[8,64]{1,0:T(8,128)} %bitcast.11, bf16[7168,1024]{1,0:T(8,128)(2,1)} %bitcast.7, bf16[7168,1024]{1,0:T(8,128)(2,1)} %bitcast.8, bf16[1024,7168]{1,0:T(8,128)(2,1)} %bitcast.9, ...), custom_call_target="tpu_custom_call" | custom-call | tf_op jit(solution)/shard_map/pallas_call | solution.py:465
  131.8 1.5 %copy.14 = bf16[64,512]{1,0:T(8,128)(2,1)} copy(bf16[64,512]{1,0:T(8,128)(2,1)} %get-tuple-element.12) | data formatting | bytes 131072
  133.2 1.3 copy.15
  134.5 1.1 copy.16
